TPU v7x, 256 devices: a whole 4x4x8 slice. The times are simulated.
256 devices in a mesh: sx: 32 (over x, y, z_lo), sy: 8 (over z_hi, core).
Axes of the slice: x: 4, y: 4, z: 8 (z_hi: 4, z_lo: 2; z = z_hi * 2 + z_lo), core: 2. Of those that a mesh axis runs over, the one named last changes fastest.
Arguments:
- weights_in: float32 [2, 32, 32, 8, 4096], P(None, None, 'sx', 'sy'), may hold values from -2.5 to 2.5
- speed_modes: float32 [4, 4], replicated, may hold values from -0.04 to 0.04
Outputs:
- weights_out: float32 [2, 32, 32, 8, 4096], P(None, None, 'sx', 'sy')
All inputs are finite; a program needn't handle non-finite values.
Results may differ from a plain program's by a relative error of at most 0.0007.
Values sent between devices are 32-bit elements; how exact they have to be, the bound alone decides.
A program may use at most 128 MiB of HBM per device.

v0:
```python
import functools

import jax
import jax.numpy as jnp
import numpy as np
from jax import lax
from jax.experimental import pallas as pl
from jax.experimental.pallas import tpu as pltpu
from jax.sharding import PartitionSpec as P

MESH = pl.DeviceIdType.MESH
GRID = 8192
CHEB = (4, 8)
SPAT = 8
FREQ = (4, 16)
COUNT = (32, 8)
MODES = 4
TILE = (8, 128)
LEVELS = ((0, 0, 0), (1, 1, 0), (0, 1, 1), (1, 2, 1), (0, 2, 2), (1, 3, 2), (0, 3, 3), (0, 4, 3))
SIN_POLY = (4.44288292, -7.30824569, 3.60635422, -0.84611165, 0.10982452)
COS_POLY = (1.4142135, -6.97885095, 5.73946038, -1.88355791, 0.31068803)


def cheb_nodes(q):
    return np.cos((2.0 * np.arange(q) + 1.0) * np.pi / (2.0 * q))


NODES = tuple(np.asarray(cheb_nodes(q), np.float32).astype(np.float64) for q in CHEB)


def child_table(q):
    z = cheb_nodes(q)
    points = -0.5 + 0.5 * z
    table = np.ones((q, q))
    for k in range(q):
        for j in range(q):
            if j != k:
                table[k, :] *= (points - z[j]) / (z[k] - z[j])
    return table


def halves(q):
    table = child_table(q)
    even = 0.5 * (table + table[::-1])[: q // 2]
    odd = 0.5 * (table - table[::-1])[: q // 2]
    return even, odd


HALVES = tuple(halves(q) for q in CHEB)


def merge(q, a, b):
    even, odd = HALVES[0 if q == 4 else 1]
    plus = [a[k] + b[q - 1 - k] for k in range(q)]
    minus = [a[k] - b[q - 1 - k] for k in range(q)]
    out = [None] * q
    for k in range(q // 2):
        e = plus[0] * float(even[k, 0])
        o = minus[0] * float(odd[k, 0])
        for j in range(1, q):
            e = e + plus[j] * float(even[k, j])
            o = o + minus[j] * float(odd[k, j])
        out[k] = e + o
        out[q - 1 - k] = e - o
    return out


def frac(v):
    return v - jnp.round(v)


def poly(coefficients, t):
    result = t * coefficients[-1] + coefficients[-2]
    for value in coefficients[-3::-1]:
        result = result * t + value
    return result


def turn(angle):
    r = frac(angle)
    t = r * r
    s = poly(SIN_POLY, t) * r
    c = poly(COS_POLY, t)
    return 1.0 - s * s, s * c


def node(e, k):
    value = jnp.float32(NODES[e][0])
    for i in range(1, CHEB[e]):
        value = jnp.where(k == i, jnp.float32(NODES[e][i]), value)
    return value


def rev(v, bits):
    result = jnp.int32(0)
    for t in range(bits):
        result = result + ((v >> t) & 1) * (1 << (bits - 1 - t))
    return result


def place(start, coord, done):
    index = start * (1 << done) + rev(coord, done)
    return (index.astype(jnp.float32) + 0.5) * (1.0 / (SPAT << done)) - 0.5


def width(e, done):
    return float(GRID // (FREQ[e] * COUNT[e]) * (1 << done))


def middle(e, high, coord, done):
    index = high * (COUNT[e] >> done) + (coord >> done)
    return (index.astype(jnp.float32) + 0.5) * width(e, done) - 0.5 * GRID


def wave(position):
    y = -position
    t = y * y
    first = y * (3.14159265 + t * (-5.16771278 + t * (2.55016404 + t * (-0.599264529 + t * (0.0821458866 - t * 0.00737043)))))
    double = first * first
    return 1.0, first, 2.0 * double - 1.0, first * (4.0 * double - 3.0)


def speed(modes, px, py):
    wx, wy = wave(px), wave(py)
    total = None
    for j in range(MODES):
        row = modes[j, 0] + modes[j, 1] * wy[1]
        for k in range(2, MODES):
            row = row + modes[j, k] * wy[k]
        row = row * wx[j] if j else row
        total = row if total is None else total + row
    return total + 0.3


def coords():
    sx, sy = lax.axis_index("sx"), lax.axis_index("sy")
    return sx // 8, sx // 2 % 4, sy // 2 * 2 + sx % 2, sy % 2


def device(x, y, z, c):
    return ((x * 4 + y) * 2 + z % 2, z // 2 * 2 + c)


def slot_of(z):
    return z % 2 * 4 + z // 2


def kernel(w_ref, modes, out_ref, given, packed, first, both, work, swapped, ready, last, table, final, local_sem,
           a_send, a_recv, c_send, c_recv, x_send, x_recv, o_send, o_recv):
    x, y, z, c = coords()
    lane = lax.broadcasted_iota(jnp.int32, TILE, 1)
    sub = lax.broadcasted_iota(jnp.int32, TILE, 0)
    low = lane < 64
    half_turn = functools.partial(pltpu.roll, shift=64, axis=1)

    load = pltpu.make_async_copy(w_ref, given, local_sem.at[0])
    load.start()
    barrier = pltpu.get_barrier_semaphore()

    @pl.loop(1, 32)
    def _(d):
        to = device(x, (y + d // 8) % 4, (z + d) % 8, c)
        pl.semaphore_signal(barrier, inc=1, device_id=to, device_id_type=MESH)

    for d in range(1, 4):
        pl.semaphore_signal(barrier, inc=1, device_id=device((x + d) % 4, y, z, c), device_id_type=MESH)
    pl.semaphore_signal(barrier, inc=1, device_id=device(x, y, z, 1 - c), device_id_type=MESH)

    load.wait()

    @pl.loop(0, 32)
    def _(k):
        for jt in range(4):
            re, im = given[0, k, jt], given[1, k, jt]
            packed[0, k, jt * 8 : jt * 8 + 8] = jnp.where(low, re, half_turn(im))
            packed[1, k, jt * 8 : jt * 8 + 8] = jnp.where(low, half_turn(re), im)

    pl.semaphore_wait(barrier, 35)

    me = y * 8 + slot_of(z)

    def first_copy(q, d):
        ty, tz = (y + d // 8) % 4, (z + d) % 8
        return pltpu.make_async_remote_copy(
            src_ref=packed.at[q, :, ty * 8 + tz],
            dst_ref=first.at[q, :, me],
            send_sem=a_send.at[q, d],
            recv_sem=a_recv.at[q, me],
            device_id=device(x, ty, tz, c),
            device_id_type=MESH,
        )

    for q in range(2):

        @pl.loop(1, 32)
        def _(d):
            first_copy(q, d).start()

        pltpu.make_async_copy(packed.at[q, :, y * 8 + z], first.at[q, :, me], a_recv.at[q, me]).start()

    def first_wait(q):
        @pl.loop(0, 32)
        def _(s):
            pltpu.make_async_copy(first.at[q, :, s], first.at[q, :, s], a_recv.at[q, s]).wait()

    def position(phase, tile):
        zh = sub & 3
        if phase == 0:
            return x * 8 + (lane >> 6) * 4 + tile * 2 + (sub >> 2), zh * 2 + c
        return tile * 16 + (sub >> 2) * 8 + (lane >> 6) * 4 + x, zh * 2 + c

    high = ((lane >> 4) & 3, lane & 15)
    chunk = y * 8 + z
    starts = [(chunk // 4, chunk % 4 * 2 + q) for q in range(2)]

    def spot(phase, tile, q, done):
        at = position(phase, tile)
        return [place(starts[q][e], at[e], done[e]) for e in range(2)]

    def make_table(n):
        e, dx, dy = LEVELS[n]
        done = (dx, dy)
        after = (dx + 1, dy) if e == 0 else (dx, dy + 1)
        phase = 0 if n < 6 else 1
        exact = n == 0
        h = [0.5 * width(i, done[i]) for i in range(2)]
        wide = n in (0, 1, 6)
        factor, inner, outer, base = {}, {}, {}, {}
        for tile in range(2):
            at = position(phase, tile)
            for q in range(2):
                new = spot(phase, tile, q, after)
                sp_new = speed(modes, *new)
                base[q, tile] = (new, sp_new)
                if n == 0:
                    factor[q, tile] = sp_new
                    outer[q, tile] = new[0] * h[0]
                    inner[q, tile] = new[1] * h[1]
                else:
                    old = spot(phase, tile, q, done)
                    factor[q, tile] = sp_new - speed(modes, *old)
                    outer[q, tile] = (new[e] - old[e]) * h[e]
        other = 1 - e
        for child in range(2):
            freq = {}
            for tile in range(2 if wide else 1):
                at = list(position(phase, tile))
                parent = [middle(i, high[i], at[i], after[i]) for i in range(2)]
                at[e] = ((at[e] >> (done[e] + 1)) * 2 + child) << done[e]
                mid = [middle(i, high[i], at[i], done[i]) for i in range(2)]
                square = 1.0 + mid[0] * mid[0] + mid[1] * mid[1]
                root = jnp.sqrt(square)
                root_parent = jnp.sqrt(1.0 + parent[0] * parent[0] + parent[1] * parent[1])
                v = (child - 0.5) * 2.0 * h[e]
                step = v * (v + 2.0 * parent[e]) / (root + root_parent)
                freq[tile] = (mid, square, root, v, step)
            constant = {}
            for tile in range(2):
                mid, square, root, v, step = freq[tile if wide else 0]
                for q in range(2):
                    new, sp_new = base[q, tile]
                    constant[q, tile] = frac(new[e] * v) + frac(sp_new * step)

            @pl.loop(0, CHEB[e])
            def _(ko):
                zo = node(e, ko)
                uo = zo * h[e]
                shift = {key: constant[key] + outer[key] * zo for key in constant}
                first_part = {t: uo * (uo + 2.0 * freq[t][0][e]) for t in freq}
                for ki in range(CHEB[other]):
                    ui = float(NODES[other][ki]) * h[other]
                    delta = {}
                    for t in freq:
                        mid, square, root = freq[t][:3]
                        total = first_part[t] + ui * (ui + 2.0 * mid[other])
                        near = square + total
                        if exact:
                            delta[t] = total / (jnp.sqrt(near) + root)
                        else:
                            delta[t] = total * pl.reciprocal(near * lax.rsqrt(near) + root, approx=True)
                    for tile in range(2):
                        for q in range(2):
                            angle = delta[tile if wide else 0] * factor[q, tile] + shift[q, tile]
                            if n == 0:
                                angle = angle + inner[q, tile] * float(NODES[other][ki])
                            cos, sin = turn(angle)
                            k = (ko, ki) if e == 0 else (ki, ko)
                            table[n, q, tile, child, k[0], k[1], 0] = cos
                            table[n, q, tile, child, k[0], k[1], 1] = sin

    def make_final():
        done = (5, 3)
        h = [0.5 * width(i, done[i]) for i in range(2)]
        at = position(1, 0)
        mid = [middle(i, high[i], at[i], done[i]) for i in range(2)]
        square = 1.0 + mid[0] * mid[0] + mid[1] * mid[1]
        root = jnp.sqrt(square)
        here = {}
        for tile in range(2):
            for q in range(2):
                px, py = spot(1, tile, q, done)
                here[q, tile] = (px * h[0], py * h[1], speed(modes, px, py))

        @pl.loop(0, CHEB[0])
        def _(ko):
            zo = node(0, ko)
            uo = zo * h[0]
            shift = {key: frac(here[key][0] * zo) for key in here}
            first_part = uo * (uo + 2.0 * mid[0])
            for ki in range(CHEB[1]):
                zi = float(NODES[1][ki])
                ui = zi * h[1]
                total = first_part + ui * (ui + 2.0 * mid[1])
                delta = total / (jnp.sqrt(square + total) + root)
                for tile in range(2):
                    for q in range(2):
                        angle = shift[q, tile] + frac(here[q, tile][1] * zi) + frac(here[q, tile][2] * delta)
                        cos, sin = turn(angle)
                        final[q, tile, ko, ki, 0] = cos
                        final[q, tile, ko, ki, 1] = sin

    def children(how, own):
        if how == "tile":
            return [(own[0], own[1])] * 2
        axis, bit, size = how
        bit_set = ((sub if axis == 0 else lane) & bit) != 0
        result = []
        for value in own:
            up = pltpu.roll(value, bit, axis)
            down = up if 2 * bit == size else pltpu.roll(value, size - bit, axis)
            result.append((jnp.where(bit_set, up, value), jnp.where(bit_set, value, down)))
        return result

    def level(n, q, how, read, write):
        e = LEVELS[n][0]
        size = CHEB[e]

        @pl.loop(0, CHEB[1 - e])
        def _(ko):
            at = [(k, ko) if e == 0 else (ko, k) for k in range(size)]
            sums = {}
            values = [read(*k) for k in at]
            for tile in range(2):
                parts = [[[], []], [[], []]]
                for i, k in enumerate(at):
                    if how is None:
                        pair_re, pair_im = values[i][tile]
                    else:
                        pair_re = children(how, values[i][0])[tile] if how == "tile" else children(how, [values[i][0][tile]])[0]
                        pair_im = children(how, values[i][1])[tile] if how == "tile" else children(how, [values[i][1][tile]])[0]
                    for child in range(2):
                        cos = table[n, q, tile, child, k[0], k[1], 0]
                        sin = table[n, q, tile, child, k[0], k[1], 1]
                        re, im = pair_re[child], pair_im[child]
                        parts[child][0].append(cos * re - sin * im)
                        parts[child][1].append(sin * re + cos * im)
                sums[tile] = [merge(size, parts[0][r], parts[1][r]) for r in range(2)]
            for tile in range(2):
                for i, k in enumerate(at):
                    write(k[0], k[1], tile, sums[tile][0][i], sums[tile][1][i])

    def read_first(q):
        def read(k0, k1):
            blocks = [first[q, k0 * 8 + k1, t * 8 : t * 8 + 8] for t in range(4)]
            turned = [half_turn(b) for b in blocks]
            re = [jnp.where(low, blocks[t], turned[2 + t]) for t in range(2)]
            im = [jnp.where(low, turned[t], blocks[2 + t]) for t in range(2)]
            return re, im

        return read

    def reader(ref, q):
        return lambda k0, k1: [[ref[q, r, k0, k1, t] for t in range(2)] for r in range(2)]

    def writer(ref, q):
        def write(k0, k1, tile, re, im):
            ref[q, 0, k0, k1, tile] = re
            ref[q, 1, k0, k1, tile] = im

        return write

    def write_both(q):
        def write(k0, k1, tile, re, im):
            both[q, c, 0, k0, k1, tile] = re
            both[q, c, 1, k0, k1, tile] = im

        return write

    def read_both(q):
        def read(k0, k1):
            return [[[both[q, child, r, k0, k1, t] for child in range(2)] for r in range(2)] for t in range(2)]

        return read

    def write_ready(q):
        def write(k0, k1, tile, re, im):
            cos, sin = final[q, tile, k0, k1, 0], final[q, tile, k0, k1, 1]
            re, im = cos * re + sin * im, cos * im - sin * re
            ready[q, 0, k0 * 8 + k1, tile * 8 : tile * 8 + 8] = jnp.where(low, re, half_turn(im))
            ready[q, 1, k0 * 8 + k1, tile * 8 : tile * 8 + 8] = jnp.where(low, half_turn(re), im)

        return write

    def core_copy(q):
        return pltpu.make_async_remote_copy(
            src_ref=both.at[q, c],
            dst_ref=both.at[q, c],
            send_sem=c_send.at[q],
            recv_sem=c_recv.at[q],
            device_id=device(x, y, z, 1 - c),
            device_id_type=MESH,
        )

    def group(q, g):
        return work.at[q, :, :, :, g // 2, pl.ds(g % 2 * 4, 4)]

    def arrived(q, g):
        return swapped.at[q, :, :, :, g // 2, pl.ds(g % 2 * 4, 4)]

    def x_copy(q, d):
        t = (x + d) % 4
        return pltpu.make_async_remote_copy(
            src_ref=group(q, t),
            dst_ref=arrived(q, x),
            send_sem=x_send.at[q, d],
            recv_sem=x_recv.at[q, x],
            device_id=device(t, y, z, c),
            device_id_type=MESH,
        )

    def x_start(q):
        for d in (2, 1, 3):
            x_copy(q, d).start()
        pltpu.make_async_copy(group(q, x), arrived(q, x), x_recv.at[q, x]).start()

    def x_wait(q):
        @pl.loop(0, 4)
        def _(g):
            pltpu.make_async_copy(arrived(q, g), arrived(q, g), x_recv.at[q, g]).wait()

    target_x = x

    def last_copy(q, d):
        tx, ty1, tz1 = (target_x + d // 8) % 4, (y // 2 + d // 4) % 2, (z // 2 + d) % 4
        to = device(tx, ty1 * 2 + x // 2, tz1 * 2 + x % 2, c)
        return ready.at[q, ty1, :, tx * 4 + tz1], to

    own_y1, own_z1 = y // 2, z // 2

    def start_last(q):
        mine = jnp.logical_and(y % 2 == x // 2, z % 2 == x % 2)

        @pl.loop(0, 32)
        def _(d):
            src, to = last_copy(q, d)
            dst = last.at[q, :, chunk]

            @pl.when(jnp.logical_not(jnp.logical_and(mine, d == 0)))
            def _():
                pltpu.make_async_remote_copy(
                    src_ref=src, dst_ref=dst, send_sem=o_send.at[q, d], recv_sem=o_recv.at[q, chunk],
                    device_id=to, device_id_type=MESH,
                ).start()

            @pl.when(jnp.logical_and(mine, d == 0))
            def _():
                pltpu.make_async_copy(src, dst, o_recv.at[q, chunk]).start()

    def wait_last_sends(q):
        mine = jnp.logical_and(y % 2 == x // 2, z % 2 == x % 2)

        @pl.loop(0, 32)
        def _(d):
            @pl.when(jnp.logical_not(jnp.logical_and(mine, d == 0)))
            def _():
                pltpu.make_async_copy(last.at[q, :, 0], last.at[q, :, 0], o_send.at[q, d]).wait()

    def wait_last(q):
        @pl.loop(0, 32)
        def _(s):
            pltpu.make_async_copy(last.at[q, :, s], last.at[q, :, s], o_recv.at[q, s]).wait()

    z0, z1, z2, y1 = (0, 4, 8), (0, 1, 8), (0, 2, 8), (1, 64, 128)

    def start_mid(q):
        first_wait(q)
        level(0, q, z0, read_first(q), write_both(q))
        core_copy(q).start()

    def mid(q):
        core_copy(q).wait()
        level(1, q, None, read_both(q), writer(work, q))
        level(2, q, "tile", reader(work, q), writer(work, q))
        level(3, q, z1, reader(work, q), writer(work, q))
        level(4, q, y1, reader(work, q), writer(work, q))
        level(5, q, z2, reader(work, q), writer(work, q))
        x_start(q)

    def end_mid(q):
        x_wait(q)
        level(6, q, z0, reader(swapped, q), writer(swapped, q))
        level(7, q, "tile", reader(swapped, q), write_ready(q))
        start_last(q)

    for n in range(6):
        make_table(n)
    start_mid(0)
    make_table(6)
    mid(0)
    make_table(7)
    make_final()
    end_mid(0)
    start_mid(1)
    mid(1)
    end_mid(1)

    for q in range(2):
        wait_last(q)

    @pl.loop(0, 32)
    def _(k):
        for jt in range(4):
            zero, one = last[0, k, jt * 8 : jt * 8 + 8], last[1, k, jt * 8 : jt * 8 + 8]
            out_ref[0, k, jt] = jnp.where(low, zero, half_turn(one))
            out_ref[1, k, jt] = jnp.where(low, half_turn(zero), one)

    for q in range(2):

        @pl.loop(1, 32)
        def _(d):
            first_copy(q, d).wait_send()

        for d in range(1, 4):
            x_copy(q, d).wait_send()
        wait_last_sends(q)


def body(weights_in, speed_modes):
    half = (2, 2, 4, 8, 2, *TILE)
    f32 = jnp.float32
    out = pl.pallas_call(
        kernel,
        out_shape=jax.ShapeDtypeStruct((2, 32, 4, *TILE), f32),
        in_specs=[pl.BlockSpec(memory_space=pltpu.HBM), pl.BlockSpec(memory_space=pltpu.SMEM)],
        out_specs=pl.BlockSpec(memory_space=pltpu.VMEM),
        scratch_shapes=[
            pltpu.VMEM((2, 32, 4, *TILE), f32),
            pltpu.VMEM((2, 32, 32, 128), f32),
            pltpu.VMEM((2, 32, 32, 128), f32),
            pltpu.VMEM((2, *half), f32),
            pltpu.VMEM(half, f32),
            pltpu.VMEM(half, f32),
            pltpu.VMEM((2, 2, 32, 16, 128), f32),
            pltpu.VMEM((2, 32, 32, 128), f32),
            pltpu.VMEM((8, 2, 2, 2, 4, 8, 2, *TILE), f32),
            pltpu.VMEM((2, 2, 4, 8, 2, *TILE), f32),
            pltpu.SemaphoreType.DMA((1,)),
            pltpu.SemaphoreType.DMA((2, 32)),
            pltpu.SemaphoreType.DMA((2, 32)),
            pltpu.SemaphoreType.DMA((2,)),
            pltpu.SemaphoreType.DMA((2,)),
            pltpu.SemaphoreType.DMA((2, 4)),
            pltpu.SemaphoreType.DMA((2, 4)),
            pltpu.SemaphoreType.DMA((2, 32)),
            pltpu.SemaphoreType.DMA((2, 32)),
        ],
        compiler_params=pltpu.CompilerParams(collective_id=0, has_side_effects=True, vmem_limit_bytes=48 << 20),
    )(weights_in.reshape(2, 32, 4, *TILE), speed_modes)
    return out.reshape(weights_in.shape)


def solution(mesh):
    placed = P(None, None, "sx", "sy", None)
    return jax.shard_map(body, mesh=mesh, in_specs=(placed, P()), out_specs=placed, check_vma=False)
```

profile of v0, /device:TPU:32, one launch (start us, length us, event | category | flops | bytes accessed | tf_op | source)
XLA Modules:
  0.0 90.8 jit_solution(2156880453561753172)
XLA Ops:
  0.0 0.0 copy-start
  0.0 1.2 %copy-done = f32[2,32,1,1,4096]{4,3,2,1,0:T(1,128)S(1)} copy-done((f32[2,32,1,1,4096]{4,3,2,1,0:T(1,128)S(1)}, f32[2,32,1,1,4096]{4,3,2,1,0:T(1,128)}, u32[]{:S(2)}) %copy-start) | copy-done | bytes 1048600
  1.2 0.0 copy-start.1
  1.2 0.7 copy-done.1
  1.9 87.9 %shard_map.28 = f32[2,32,4,8,128]{4,3,2,1,0:T(8,128)S(1)} custom-call(f32[2,32,4,8,128]{4,3,2,1,0:T(8,128)S(1)} %bitcast.3, f32[4,4]{1,0:T(4,128)S(1)} %copy-done.1), custom_call_target="tpu_custom_call" | custom-call | tf_op jit(solution)/shard_map/pallas_call | solution.py:541
  89.8 1.0 %copy.5 = f32[2,32,1,1,4096]{4,3,2,1,0:T(1,128)} copy(f32[2,32,1,1,4096]{4,3,2,1,0:T(1,128)S(1)} %bitcast.2) | data formatting | bytes 2097152
Async XLA Ops:
  0.0 1.2 %copy-start = (f32[2,32,1,1,4096]{4,3,2,1,0:T(1,128)S(1)}, f32[2,32,1,1,4096]{4,3,2,1,0:T(1,128)}, u32[]{:S(2)}) copy-start(f32[2,32,1,1,4096]{4,3,2,1,0:T(1,128)} %param.2) | copy-start | bytes 3145732
  1.2 0.7 copy-start.1
where the time goes:
time: 92.6 us; the launch traced here: 90.8 us
  Pallas kernels  87.9 us (95%)
  local copies, waits for them, and re-layouts  2.88 us (3%)
    pallas_call x1, Pallas kernels, body(): pl.pallas_call(kernel, out_shape=jax.ShapeDtypeStruct((2, 32, 4, *TILE),...  87.9 us
    unnamed x5, local copies, waits for them, and re-layouts  2.88 us

commit v1 on v0

--- a/solution.py
+++ b/solution.py
@@ -134,18 +134,18 @@
 
 def coords():
     sx, sy = lax.axis_index("sx"), lax.axis_index("sy")
-    return sx // 8, sx // 2 % 4, sy // 2 * 2 + sx % 2, sy % 2
+    return sx >> 3, (sx >> 1) & 3, (sy >> 1) * 2 + (sx & 1), sy & 1
 
 
 def device(x, y, z, c):
-    return ((x * 4 + y) * 2 + z % 2, z // 2 * 2 + c)
+    return ((x * 4 + y) * 2 + (z & 1), (z >> 1) * 2 + c)
 
 
 def slot_of(z):
-    return z % 2 * 4 + z // 2
-
-
-def kernel(w_ref, modes, out_ref, given, packed, first, both, work, swapped, ready, last, table, final, local_sem,
+    return (z & 1) * 4 + (z >> 1)
+
+
+def kernel(w_ref, modes, out_ref, packed, first, both, work, swapped, ready, last, table, final,
            a_send, a_recv, c_send, c_recv, x_send, x_recv, o_send, o_recv):
     x, y, z, c = coords()
     lane = lax.broadcasted_iota(jnp.int32, TILE, 1)
@@ -153,25 +153,20 @@
     low = lane < 64
     half_turn = functools.partial(pltpu.roll, shift=64, axis=1)
 
-    load = pltpu.make_async_copy(w_ref, given, local_sem.at[0])
-    load.start()
     barrier = pltpu.get_barrier_semaphore()
 
-    @pl.loop(1, 32)
-    def _(d):
-        to = device(x, (y + d // 8) % 4, (z + d) % 8, c)
+    for d in range(1, 32):
+        to = device(x, (y + (d >> 3)) & 3, (z + d) & 7, c)
         pl.semaphore_signal(barrier, inc=1, device_id=to, device_id_type=MESH)
 
     for d in range(1, 4):
-        pl.semaphore_signal(barrier, inc=1, device_id=device((x + d) % 4, y, z, c), device_id_type=MESH)
+        pl.semaphore_signal(barrier, inc=1, device_id=device((x + d) & 3, y, z, c), device_id_type=MESH)
     pl.semaphore_signal(barrier, inc=1, device_id=device(x, y, z, 1 - c), device_id_type=MESH)
-
-    load.wait()
 
     @pl.loop(0, 32)
     def _(k):
         for jt in range(4):
-            re, im = given[0, k, jt], given[1, k, jt]
+            re, im = w_ref[0, k, jt], w_ref[1, k, jt]
             packed[0, k, jt * 8 : jt * 8 + 8] = jnp.where(low, re, half_turn(im))
             packed[1, k, jt * 8 : jt * 8 + 8] = jnp.where(low, half_turn(re), im)
 
@@ -180,7 +175,7 @@
     me = y * 8 + slot_of(z)
 
     def first_copy(q, d):
-        ty, tz = (y + d // 8) % 4, (z + d) % 8
+        ty, tz = (y + (d >> 3)) & 3, (z + d) & 7
         return pltpu.make_async_remote_copy(
             src_ref=packed.at[q, :, ty * 8 + tz],
             dst_ref=first.at[q, :, me],
@@ -190,24 +185,38 @@
             device_id_type=MESH,
         )
 
-    for q in range(2):
-
+    def first_start(q, begin, count):
+        for d in range(count):
+            first_copy(q, begin + d).start()
+
+    def first_own(q):
+        pltpu.make_async_copy(packed.at[q, :, y * 8 + z], first.at[q, :, me], a_recv.at[q, me]).start()
+
+    def first_sent(q):
         @pl.loop(1, 32)
         def _(d):
-            first_copy(q, d).start()
-
-        pltpu.make_async_copy(packed.at[q, :, y * 8 + z], first.at[q, :, me], a_recv.at[q, me]).start()
+            first_copy(q, d).wait_send()
+
+    first_start(0, 1, 31)
+    first_start(1, 1, 31)
+    first_own(0)
+    first_own(1)
 
     def first_wait(q):
         @pl.loop(0, 32)
         def _(s):
             pltpu.make_async_copy(first.at[q, :, s], first.at[q, :, s], a_recv.at[q, s]).wait()
 
+    def group_of(to):
+        return (((to >> 1) + y) & 1) * 2 + ((to + z) & 1)
+
+    mine = group_of(x)
+
     def position(phase, tile):
         zh = sub & 3
         if phase == 0:
             return x * 8 + (lane >> 6) * 4 + tile * 2 + (sub >> 2), zh * 2 + c
-        return tile * 16 + (sub >> 2) * 8 + (lane >> 6) * 4 + x, zh * 2 + c
+        return tile * 16 + (sub >> 2) * 8 + (lane >> 6) * 4 + mine, zh * 2 + c
 
     high = ((lane >> 4) & 3, lane & 15)
     chunk = y * 8 + z
@@ -331,7 +340,7 @@
             result.append((jnp.where(bit_set, up, value), jnp.where(bit_set, value, down)))
         return result
 
-    def level(n, q, how, read, write):
+    def level(n, q, how, read, write, then=None):
         e = LEVELS[n][0]
         size = CHEB[e]
 
@@ -358,6 +367,8 @@
             for tile in range(2):
                 for i, k in enumerate(at):
                     write(k[0], k[1], tile, sums[tile][0][i], sums[tile][1][i])
+            if then is not None:
+                then(ko)
 
     def read_first(q):
         def read(k0, k1):
@@ -411,69 +422,66 @@
             device_id_type=MESH,
         )
 
-    def group(q, g):
-        return work.at[q, :, :, :, g // 2, pl.ds(g % 2 * 4, 4)]
-
-    def arrived(q, g):
-        return swapped.at[q, :, :, :, g // 2, pl.ds(g % 2 * 4, 4)]
-
-    def x_copy(q, d):
-        t = (x + d) % 4
+    def group(q, g, k0):
+        return work.at[q, :, k0, :, g >> 1, pl.ds((g & 1) * 4, 4)]
+
+    def arrived(q, g, k0):
+        return swapped.at[q, :, k0, :, g >> 1, pl.ds((g & 1) * 4, 4)]
+
+    def x_copy(q, d, k0):
+        t = (x + d) & 3
         return pltpu.make_async_remote_copy(
-            src_ref=group(q, t),
-            dst_ref=arrived(q, x),
-            send_sem=x_send.at[q, d],
-            recv_sem=x_recv.at[q, x],
+            src_ref=group(q, group_of(t), k0),
+            dst_ref=arrived(q, x, k0),
+            send_sem=x_send.at[q, d, k0],
+            recv_sem=x_recv.at[q, x, k0],
             device_id=device(t, y, z, c),
             device_id_type=MESH,
         )
 
-    def x_start(q):
-        for d in (2, 1, 3):
-            x_copy(q, d).start()
-        pltpu.make_async_copy(group(q, x), arrived(q, x), x_recv.at[q, x]).start()
-
     def x_wait(q):
-        @pl.loop(0, 4)
-        def _(g):
-            pltpu.make_async_copy(arrived(q, g), arrived(q, g), x_recv.at[q, g]).wait()
-
-    target_x = x
+        @pl.loop(0, 16)
+        def _(i):
+            part = arrived(q, i >> 2, i & 3)
+            pltpu.make_async_copy(part, part, x_recv.at[q, i >> 2, i & 3]).wait()
 
     def last_copy(q, d):
-        tx, ty1, tz1 = (target_x + d // 8) % 4, (y // 2 + d // 4) % 2, (z // 2 + d) % 4
-        to = device(tx, ty1 * 2 + x // 2, tz1 * 2 + x % 2, c)
+        tx, ty1, tz1 = (x + (d >> 3)) & 3, ((y >> 1) + (d >> 2)) & 1, ((z >> 1) + d) & 3
+        to = device(tx, ty1 * 2 + (mine >> 1), tz1 * 2 + (mine & 1), c)
         return ready.at[q, ty1, :, tx * 4 + tz1], to
 
-    own_y1, own_z1 = y // 2, z // 2
-
-    def start_last(q):
-        mine = jnp.logical_and(y % 2 == x // 2, z % 2 == x % 2)
-
-        @pl.loop(0, 32)
+    def last_remote(q, d):
+        src, to = last_copy(q, d)
+        return pltpu.make_async_remote_copy(
+            src_ref=src,
+            dst_ref=last.at[q, :, chunk],
+            send_sem=o_send.at[q, d],
+            recv_sem=o_recv.at[q, chunk],
+            device_id=to,
+            device_id_type=MESH,
+        )
+
+    def start_last(q, begin, count):
+        for d in range(count):
+            last_remote(q, begin + d).start()
+
+    def start_last_own(q):
+        @pl.when(x != 0)
+        def _():
+            last_remote(q, 0).start()
+
+        @pl.when(x == 0)
+        def _():
+            pltpu.make_async_copy(last_copy(q, 0)[0], last.at[q, :, chunk], o_recv.at[q, chunk]).start()
+
+    def wait_last_sends(q):
+        @pl.loop(1, 32)
         def _(d):
-            src, to = last_copy(q, d)
-            dst = last.at[q, :, chunk]
-
-            @pl.when(jnp.logical_not(jnp.logical_and(mine, d == 0)))
-            def _():
-                pltpu.make_async_remote_copy(
-                    src_ref=src, dst_ref=dst, send_sem=o_send.at[q, d], recv_sem=o_recv.at[q, chunk],
-                    device_id=to, device_id_type=MESH,
-                ).start()
-
-            @pl.when(jnp.logical_and(mine, d == 0))
-            def _():
-                pltpu.make_async_copy(src, dst, o_recv.at[q, chunk]).start()
-
-    def wait_last_sends(q):
-        mine = jnp.logical_and(y % 2 == x // 2, z % 2 == x % 2)
-
-        @pl.loop(0, 32)
-        def _(d):
-            @pl.when(jnp.logical_not(jnp.logical_and(mine, d == 0)))
-            def _():
-                pltpu.make_async_copy(last.at[q, :, 0], last.at[q, :, 0], o_send.at[q, d]).wait()
+            last_remote(q, d).wait_send()
+
+        @pl.when(x != 0)
+        def _():
+            last_remote(q, 0).wait_send()
 
     def wait_last(q):
         @pl.loop(0, 32)
@@ -482,38 +490,48 @@
 
     z0, z1, z2, y1 = (0, 4, 8), (0, 1, 8), (0, 2, 8), (1, 64, 128)
 
-    def start_mid(q):
+    def open_half(q):
         first_wait(q)
         level(0, q, z0, read_first(q), write_both(q))
         core_copy(q).start()
 
-    def mid(q):
+    def middle_half(q):
         core_copy(q).wait()
         level(1, q, None, read_both(q), writer(work, q))
         level(2, q, "tile", reader(work, q), writer(work, q))
         level(3, q, z1, reader(work, q), writer(work, q))
         level(4, q, y1, reader(work, q), writer(work, q))
-        level(5, q, z2, reader(work, q), writer(work, q))
-        x_start(q)
-
-    def end_mid(q):
+
+    def swap_half(q, more, done, each):
+        def send(k0):
+            for n, d in enumerate((2, 1, 3)):
+                x_copy(q, d, k0).start()
+                begin, end = n * each // 3, (n + 1) * each // 3
+                more(done + k0 * each + begin, end - begin)
+            pltpu.make_async_copy(group(q, mine, k0), arrived(q, x, k0), x_recv.at[q, x, k0]).start()
+
+        level(5, q, z2, reader(work, q), writer(work, q), send)
+
+    def second_half(q):
         x_wait(q)
         level(6, q, z0, reader(swapped, q), writer(swapped, q))
         level(7, q, "tile", reader(swapped, q), write_ready(q))
-        start_last(q)
-
-    for n in range(6):
+
+    for n in range(8):
         make_table(n)
-    start_mid(0)
-    make_table(6)
-    mid(0)
-    make_table(7)
     make_final()
-    end_mid(0)
-    start_mid(1)
-    mid(1)
-    end_mid(1)
-
+    open_half(0)
+    middle_half(0)
+    swap_half(0, (lambda b, n: None), 0, 0)
+    open_half(1)
+    middle_half(1)
+    swap_half(1, (lambda b, n: None), 0, 0)
+    second_half(0)
+    start_last(0, 1, 31)
+    start_last_own(0)
+    second_half(1)
+    start_last(1, 1, 31)
+    start_last_own(1)
     for q in range(2):
         wait_last(q)
 
@@ -525,13 +543,10 @@
             out_ref[1, k, jt] = jnp.where(low, half_turn(zero), one)
 
     for q in range(2):
-
-        @pl.loop(1, 32)
-        def _(d):
-            first_copy(q, d).wait_send()
-
+        first_sent(q)
         for d in range(1, 4):
-            x_copy(q, d).wait_send()
+            for k0 in range(4):
+                x_copy(q, d, k0).wait_send()
         wait_last_sends(q)
 
 
@@ -541,10 +556,9 @@
     out = pl.pallas_call(
         kernel,
         out_shape=jax.ShapeDtypeStruct((2, 32, 4, *TILE), f32),
-        in_specs=[pl.BlockSpec(memory_space=pltpu.HBM), pl.BlockSpec(memory_space=pltpu.SMEM)],
+        in_specs=[pl.BlockSpec(memory_space=pltpu.VMEM), pl.BlockSpec(memory_space=pltpu.SMEM)],
         out_specs=pl.BlockSpec(memory_space=pltpu.VMEM),
         scratch_shapes=[
-            pltpu.VMEM((2, 32, 4, *TILE), f32),
             pltpu.VMEM((2, 32, 32, 128), f32),
             pltpu.VMEM((2, 32, 32, 128), f32),
             pltpu.VMEM((2, *half), f32),
@@ -554,13 +568,12 @@
             pltpu.VMEM((2, 32, 32, 128), f32),
             pltpu.VMEM((8, 2, 2, 2, 4, 8, 2, *TILE), f32),
             pltpu.VMEM((2, 2, 4, 8, 2, *TILE), f32),
-            pltpu.SemaphoreType.DMA((1,)),
             pltpu.SemaphoreType.DMA((2, 32)),
             pltpu.SemaphoreType.DMA((2, 32)),
             pltpu.SemaphoreType.DMA((2,)),
             pltpu.SemaphoreType.DMA((2,)),
-            pltpu.SemaphoreType.DMA((2, 4)),
-            pltpu.SemaphoreType.DMA((2, 4)),
+            pltpu.SemaphoreType.DMA((2, 4, 4)),
+            pltpu.SemaphoreType.DMA((2, 4, 4)),
             pltpu.SemaphoreType.DMA((2, 32)),
             pltpu.SemaphoreType.DMA((2, 32)),
         ],

time: 92.6 us -> 81.6 us (0.88); the launches traced: 90.8 us -> 81.2 us
  Pallas kernels: 87.9 us -> 78.3 us
    pallas_call x1, Pallas kernels: 87.9 us -> 78.3 us  [body(): pl.pallas_call(kernel, out_shape=jax.ShapeDtypeStruct((2, 32, 4, *TILE),...]
where the time goes in v1:
time: 81.6 us; the launch traced here: 81.2 us
  Pallas kernels  78.3 us (96%)
  local copies, waits for them, and re-layouts  2.88 us (4%)
    pallas_call x1, Pallas kernels, body(): pl.pallas_call(kernel, out_shape=jax.ShapeDtypeStruct((2, 32, 4, *TILE),...  78.3 us
    unnamed x5, local copies, waits for them, and re-layouts  2.88 us

profile of v1, /device:TPU:32, one launch (start us, length us, event | category | flops | bytes accessed | tf_op | source)
XLA Modules:
  0.0 81.2 jit_solution(8950459609975685371)
XLA Ops:
  0.0 0.0 copy-start
  0.0 1.2 %copy-done = f32[2,32,1,1,4096]{4,3,2,1,0:T(1,128)S(1)} copy-done((f32[2,32,1,1,4096]{4,3,2,1,0:T(1,128)S(1)}, f32[2,32,1,1,4096]{4,3,2,1,0:T(1,128)}, u32[]{:S(2)}) %copy-start) | copy-done | bytes 1048600
  1.2 0.0 copy-start.1
  1.2 0.7 copy-done.1
  1.9 78.3 %shard_map.28 = f32[2,32,4,8,128]{4,3,2,1,0:T(8,128)S(1)} custom-call(f32[2,32,4,8,128]{4,3,2,1,0:T(8,128)S(1)} %bitcast.3, f32[4,4]{1,0:T(4,128)S(1)} %copy-done.1), custom_call_target="tpu_custom_call" | custom-call | tf_op jit(solution)/shard_map/pallas_call | solution.py:556
  80.2 1.0 %copy.5 = f32[2,32,1,1,4096]{4,3,2,1,0:T(1,128)} copy(f32[2,32,1,1,4096]{4,3,2,1,0:T(1,128)S(1)} %bitcast.2) | data formatting | bytes 2097152
Async XLA Ops:
  0.0 1.2 %copy-start = (f32[2,32,1,1,4096]{4,3,2,1,0:T(1,128)S(1)}, f32[2,32,1,1,4096]{4,3,2,1,0:T(1,128)}, u32[]{:S(2)}) copy-start(f32[2,32,1,1,4096]{4,3,2,1,0:T(1,128)} %param.2) | copy-start | bytes 3145732
  1.2 0.7 copy-start.1

commit v2 on v1

--- a/solution.py
+++ b/solution.py
@@ -155,7 +155,7 @@
 
     barrier = pltpu.get_barrier_semaphore()
 
-    for d in range(1, 32):
+    for d in sorted(range(1, 32), key=lambda d: -min(d & 7, 8 - (d & 7)) - min(d >> 3, 4 - (d >> 3))):
         to = device(x, (y + (d >> 3)) & 3, (z + d) & 7, c)
         pl.semaphore_signal(barrier, inc=1, device_id=to, device_id_type=MESH)
 
@@ -340,12 +340,13 @@
             result.append((jnp.where(bit_set, up, value), jnp.where(bit_set, value, down)))
         return result
 
-    def level(n, q, how, read, write, then=None):
+    def level(n, q, how, read, write, begin=0, count=None):
         e = LEVELS[n][0]
         size = CHEB[e]
 
-        @pl.loop(0, CHEB[1 - e])
-        def _(ko):
+        @pl.loop(0, CHEB[1 - e] if count is None else count)
+        def _(step):
+            ko = begin + step
             at = [(k, ko) if e == 0 else (ko, k) for k in range(size)]
             sums = {}
             values = [read(*k) for k in at]
@@ -367,8 +368,6 @@
             for tile in range(2):
                 for i, k in enumerate(at):
                     write(k[0], k[1], tile, sums[tile][0][i], sums[tile][1][i])
-            if then is not None:
-                then(ko)
 
     def read_first(q):
         def read(k0, k1):
@@ -407,8 +406,8 @@
         def write(k0, k1, tile, re, im):
             cos, sin = final[q, tile, k0, k1, 0], final[q, tile, k0, k1, 1]
             re, im = cos * re + sin * im, cos * im - sin * re
-            ready[q, 0, k0 * 8 + k1, tile * 8 : tile * 8 + 8] = jnp.where(low, re, half_turn(im))
-            ready[q, 1, k0 * 8 + k1, tile * 8 : tile * 8 + 8] = jnp.where(low, half_turn(re), im)
+            ready[q, 0, k1 * 4 + k0, tile * 8 : tile * 8 + 8] = jnp.where(low, re, half_turn(im))
+            ready[q, 1, k1 * 4 + k0, tile * 8 : tile * 8 + 8] = jnp.where(low, half_turn(re), im)
 
         return write
 
@@ -422,71 +421,77 @@
             device_id_type=MESH,
         )
 
-    def group(q, g, k0):
-        return work.at[q, :, k0, :, g >> 1, pl.ds((g & 1) * 4, 4)]
-
-    def arrived(q, g, k0):
-        return swapped.at[q, :, k0, :, g >> 1, pl.ds((g & 1) * 4, 4)]
-
-    def x_copy(q, d, k0):
+    def group(q, g, i):
+        return work.at[q, :, :, pl.ds(2 * i, 2), g >> 1, pl.ds((g & 1) * 4, 4)]
+
+    def arrived(q, g, i):
+        return swapped.at[q, :, :, pl.ds(2 * i, 2), g >> 1, pl.ds((g & 1) * 4, 4)]
+
+    def x_copy(q, d, i):
         t = (x + d) & 3
         return pltpu.make_async_remote_copy(
-            src_ref=group(q, group_of(t), k0),
-            dst_ref=arrived(q, x, k0),
-            send_sem=x_send.at[q, d, k0],
-            recv_sem=x_recv.at[q, x, k0],
+            src_ref=group(q, group_of(t), i),
+            dst_ref=arrived(q, x, i),
+            send_sem=x_send.at[q, d, i],
+            recv_sem=x_recv.at[q, x, i],
             device_id=device(t, y, z, c),
             device_id_type=MESH,
         )
 
-    def x_wait(q):
-        @pl.loop(0, 16)
-        def _(i):
-            part = arrived(q, i >> 2, i & 3)
-            pltpu.make_async_copy(part, part, x_recv.at[q, i >> 2, i & 3]).wait()
-
-    def last_copy(q, d):
+    def x_wait(q, i):
+        for g in range(4):
+            part = arrived(q, g, i)
+            pltpu.make_async_copy(part, part, x_recv.at[q, g, i]).wait()
+
+    PARTS = ((0, 0, 32), (1, 0, 16), (1, 16, 16))
+
+    def last_copy(part, d):
+        q, row, count = PARTS[part]
+        rows = pl.ds(row, count)
         tx, ty1, tz1 = (x + (d >> 3)) & 3, ((y >> 1) + (d >> 2)) & 1, ((z >> 1) + d) & 3
         to = device(tx, ty1 * 2 + (mine >> 1), tz1 * 2 + (mine & 1), c)
-        return ready.at[q, ty1, :, tx * 4 + tz1], to
-
-    def last_remote(q, d):
-        src, to = last_copy(q, d)
+        return ready.at[q, ty1, rows, tx * 4 + tz1], to
+
+    def landing(part, slot):
+        q, row, count = PARTS[part]
+        return last.at[q, pl.ds(row, count), slot]
+
+    def last_remote(part, d):
+        src, to = last_copy(part, d)
         return pltpu.make_async_remote_copy(
             src_ref=src,
-            dst_ref=last.at[q, :, chunk],
-            send_sem=o_send.at[q, d],
-            recv_sem=o_recv.at[q, chunk],
+            dst_ref=landing(part, chunk),
+            send_sem=o_send.at[part, d],
+            recv_sem=o_recv.at[part, chunk],
             device_id=to,
             device_id_type=MESH,
         )
 
-    def start_last(q, begin, count):
-        for d in range(count):
-            last_remote(q, begin + d).start()
-
-    def start_last_own(q):
+    def start_last(part):
+        for d in range(1, 32):
+            last_remote(part, d).start()
+
         @pl.when(x != 0)
         def _():
-            last_remote(q, 0).start()
+            last_remote(part, 0).start()
 
         @pl.when(x == 0)
         def _():
-            pltpu.make_async_copy(last_copy(q, 0)[0], last.at[q, :, chunk], o_recv.at[q, chunk]).start()
-
-    def wait_last_sends(q):
+            pltpu.make_async_copy(last_copy(part, 0)[0], landing(part, chunk), o_recv.at[part, chunk]).start()
+
+    def wait_last_sends(part):
         @pl.loop(1, 32)
         def _(d):
-            last_remote(q, d).wait_send()
+            last_remote(part, d).wait_send()
 
         @pl.when(x != 0)
         def _():
-            last_remote(q, 0).wait_send()
-
-    def wait_last(q):
+            last_remote(part, 0).wait_send()
+
+    def wait_last(part):
         @pl.loop(0, 32)
         def _(s):
-            pltpu.make_async_copy(last.at[q, :, s], last.at[q, :, s], o_recv.at[q, s]).wait()
+            pltpu.make_async_copy(landing(part, s), landing(part, s), o_recv.at[part, s]).wait()
 
     z0, z1, z2, y1 = (0, 4, 8), (0, 1, 8), (0, 2, 8), (1, 64, 128)
 
@@ -502,52 +507,54 @@
         level(3, q, z1, reader(work, q), writer(work, q))
         level(4, q, y1, reader(work, q), writer(work, q))
 
-    def swap_half(q, more, done, each):
-        def send(k0):
-            for n, d in enumerate((2, 1, 3)):
-                x_copy(q, d, k0).start()
-                begin, end = n * each // 3, (n + 1) * each // 3
-                more(done + k0 * each + begin, end - begin)
-            pltpu.make_async_copy(group(q, mine, k0), arrived(q, x, k0), x_recv.at[q, x, k0]).start()
-
-        level(5, q, z2, reader(work, q), writer(work, q), send)
-
-    def second_half(q):
-        x_wait(q)
-        level(6, q, z0, reader(swapped, q), writer(swapped, q))
-        level(7, q, "tile", reader(swapped, q), write_ready(q))
+    def swap_half(q):
+        level(5, q, z2, reader(work, q), writer(work, q))
+        for i in range(4):
+            for d in (2, 1, 3):
+                x_copy(q, d, i).start()
+            pltpu.make_async_copy(group(q, mine, i), arrived(q, x, i), x_recv.at[q, x, i]).start()
+
+    def second_half(q, begin, end):
+        @pl.loop(begin, end)
+        def _(i):
+            x_wait(q, i)
+            level(6, q, z0, reader(swapped, q), writer(swapped, q), 2 * i, 2)
+            level(7, q, "tile", reader(swapped, q), write_ready(q), 2 * i, 2)
 
     for n in range(8):
         make_table(n)
     make_final()
     open_half(0)
     middle_half(0)
-    swap_half(0, (lambda b, n: None), 0, 0)
+    swap_half(0)
     open_half(1)
+    second_half(0, 0, 4)
     middle_half(1)
-    swap_half(1, (lambda b, n: None), 0, 0)
-    second_half(0)
-    start_last(0, 1, 31)
-    start_last_own(0)
-    second_half(1)
-    start_last(1, 1, 31)
-    start_last_own(1)
-    for q in range(2):
-        wait_last(q)
-
-    @pl.loop(0, 32)
-    def _(k):
-        for jt in range(4):
-            zero, one = last[0, k, jt * 8 : jt * 8 + 8], last[1, k, jt * 8 : jt * 8 + 8]
-            out_ref[0, k, jt] = jnp.where(low, zero, half_turn(one))
-            out_ref[1, k, jt] = jnp.where(low, half_turn(zero), one)
+    swap_half(1)
+    start_last(0)
+    second_half(1, 0, 2)
+    start_last(1)
+    second_half(1, 2, 4)
+    start_last(2)
+
+    for part in range(3):
+        wait_last(part)
+
+    @pl.loop(0, 8)
+    def _(k1):
+        for k0 in range(4):
+            for jt in range(4):
+                zero, one = last[0, k1 * 4 + k0, jt * 8 : jt * 8 + 8], last[1, k1 * 4 + k0, jt * 8 : jt * 8 + 8]
+                out_ref[0, k0 * 8 + k1, jt] = jnp.where(low, zero, half_turn(one))
+                out_ref[1, k0 * 8 + k1, jt] = jnp.where(low, half_turn(zero), one)
 
     for q in range(2):
         first_sent(q)
         for d in range(1, 4):
-            for k0 in range(4):
-                x_copy(q, d, k0).wait_send()
-        wait_last_sends(q)
+            for i in range(4):
+                x_copy(q, d, i).wait_send()
+    for part in range(3):
+        wait_last_sends(part)
 
 
 def body(weights_in, speed_modes):
@@ -574,8 +581,8 @@
             pltpu.SemaphoreType.DMA((2,)),
             pltpu.SemaphoreType.DMA((2, 4, 4)),
             pltpu.SemaphoreType.DMA((2, 4, 4)),
-            pltpu.SemaphoreType.DMA((2, 32)),
-            pltpu.SemaphoreType.DMA((2, 32)),
+            pltpu.SemaphoreType.DMA((3, 32)),
+            pltpu.SemaphoreType.DMA((3, 32)),
         ],
         compiler_params=pltpu.CompilerParams(collective_id=0, has_side_effects=True, vmem_limit_bytes=48 << 20),
     )(weights_in.reshape(2, 32, 4, *TILE), speed_modes)

time: 81.6 us -> 79.4 us (0.973)
  Pallas kernels: 78.3 us -> 76.4 us
    pallas_call x1, Pallas kernels: 78.3 us -> 76.4 us  [body(): pl.pallas_call(kernel, out_shape=jax.ShapeDtypeStruct((2, 32, 4, *TILE),...]
where the time goes in v2:
time: 79.4 us; the launch traced here: 79.3 us
  Pallas kernels  76.4 us (96%)
  local copies, waits for them, and re-layouts  2.88 us (4%)
    pallas_call x1, Pallas kernels, body(): pl.pallas_call(kernel, out_shape=jax.ShapeDtypeStruct((2, 32, 4, *TILE),...  76.4 us
    unnamed x5, local copies, waits for them, and re-layouts  2.88 us

profile of v2, /device:TPU:32, one launch (start us, length us, event | category | flops | bytes accessed | tf_op | source)
XLA Modules:
  0.0 79.3 jit_solution(9750926675376342808)
XLA Ops:
  0.0 0.0 copy-start
  0.0 1.2 %copy-done = f32[2,32,1,1,4096]{4,3,2,1,0:T(1,128)S(1)} copy-done((f32[2,32,1,1,4096]{4,3,2,1,0:T(1,128)S(1)}, f32[2,32,1,1,4096]{4,3,2,1,0:T(1,128)}, u32[]{:S(2)}) %copy-start) | copy-done | bytes 1048600
  1.2 0.0 copy-start.1
  1.2 0.7 copy-done.1
  1.9 76.4 %shard_map.28 = f32[2,32,4,8,128]{4,3,2,1,0:T(8,128)S(1)} custom-call(f32[2,32,4,8,128]{4,3,2,1,0:T(8,128)S(1)} %bitcast.3, f32[4,4]{1,0:T(4,128)S(1)} %copy-done.1), custom_call_target="tpu_custom_call" | custom-call | tf_op jit(solution)/shard_map/pallas_call | solution.py:563
  78.3 1.0 %copy.5 = f32[2,32,1,1,4096]{4,3,2,1,0:T(1,128)} copy(f32[2,32,1,1,4096]{4,3,2,1,0:T(1,128)S(1)} %bitcast.2) | data formatting | bytes 2097152
Async XLA Ops:
  0.0 1.2 %copy-start = (f32[2,32,1,1,4096]{4,3,2,1,0:T(1,128)S(1)}, f32[2,32,1,1,4096]{4,3,2,1,0:T(1,128)}, u32[]{:S(2)}) copy-start(f32[2,32,1,1,4096]{4,3,2,1,0:T(1,128)} %param.2) | copy-start | bytes 3145732
  1.2 0.7 copy-start.1

commit v3 on v2

--- a/solution.py
+++ b/solution.py
@@ -530,8 +530,8 @@
     open_half(1)
     second_half(0, 0, 4)
     middle_half(1)
+    start_last(0)
     swap_half(1)
-    start_last(0)
     second_half(1, 0, 2)
     start_last(1)
     second_half(1, 2, 4)

time: 79.4 us -> 79 us (level)
  no operation moved by 1% of the time
where the time goes in v3:
time: 79 us; the launch traced here: 78.9 us
  Pallas kernels  76 us (96%)
  local copies, waits for them, and re-layouts  2.88 us (4%)
    pallas_call x1, Pallas kernels, body(): pl.pallas_call(kernel, out_shape=jax.ShapeDtypeStruct((2, 32, 4, *TILE),...  76 us
    unnamed x5, local copies, waits for them, and re-layouts  2.88 us

profile of v3, /device:TPU:32, one launch (start us, length us, event | category | flops | bytes accessed | tf_op | source)
XLA Modules:
  0.0 78.9 jit_solution(15014467375453865926)
XLA Ops:
  0.0 0.0 copy-start
  0.0 1.2 %copy-done = f32[2,32,1,1,4096]{4,3,2,1,0:T(1,128)S(1)} copy-done((f32[2,32,1,1,4096]{4,3,2,1,0:T(1,128)S(1)}, f32[2,32,1,1,4096]{4,3,2,1,0:T(1,128)}, u32[]{:S(2)}) %copy-start) | copy-done | bytes 1048600
  1.2 0.0 copy-start.1
  1.2 0.7 copy-done.1
  1.9 76.0 %shard_map.28 = f32[2,32,4,8,128]{4,3,2,1,0:T(8,128)S(1)} custom-call(f32[2,32,4,8,128]{4,3,2,1,0:T(8,128)S(1)} %bitcast.3, f32[4,4]{1,0:T(4,128)S(1)} %copy-done.1), custom_call_target="tpu_custom_call" | custom-call | tf_op jit(solution)/shard_map/pallas_call | solution.py:563
  77.9 1.0 %copy.5 = f32[2,32,1,1,4096]{4,3,2,1,0:T(1,128)} copy(f32[2,32,1,1,4096]{4,3,2,1,0:T(1,128)S(1)} %bitcast.2) | data formatting | bytes 2097152
Async XLA Ops:
  0.0 1.2 %copy-start = (f32[2,32,1,1,4096]{4,3,2,1,0:T(1,128)S(1)}, f32[2,32,1,1,4096]{4,3,2,1,0:T(1,128)}, u32[]{:S(2)}) copy-start(f32[2,32,1,1,4096]{4,3,2,1,0:T(1,128)} %param.2) | copy-start | bytes 3145732
  1.2 0.7 copy-start.1

commit v4 on v3

--- a/solution.py
+++ b/solution.py
@@ -537,16 +537,17 @@
     second_half(1, 2, 4)
     start_last(2)
 
-    for part in range(3):
+    wait_last(0)
+    for part in (1, 2):
         wait_last(part)
 
-    @pl.loop(0, 8)
-    def _(k1):
-        for k0 in range(4):
-            for jt in range(4):
-                zero, one = last[0, k1 * 4 + k0, jt * 8 : jt * 8 + 8], last[1, k1 * 4 + k0, jt * 8 : jt * 8 + 8]
-                out_ref[0, k0 * 8 + k1, jt] = jnp.where(low, zero, half_turn(one))
-                out_ref[1, k0 * 8 + k1, jt] = jnp.where(low, half_turn(zero), one)
+        @pl.loop(part * 4 - 4, part * 4)
+        def _(k1):
+            for k0 in range(4):
+                for jt in range(4):
+                    zero, one = last[0, k1 * 4 + k0, jt * 8 : jt * 8 + 8], last[1, k1 * 4 + k0, jt * 8 : jt * 8 + 8]
+                    out_ref[0, k0 * 8 + k1, jt] = jnp.where(low, zero, half_turn(one))
+                    out_ref[1, k0 * 8 + k1, jt] = jnp.where(low, half_turn(zero), one)
 
     for q in range(2):
         first_sent(q)

time: 79 us -> 78.6 us (level)
  no operation moved by 1% of the time
where the time goes in v4:
time: 78.6 us; the launch traced here: 78.5 us
  Pallas kernels  75.6 us (96%)
  local copies, waits for them, and re-layouts  2.88 us (4%)
    pallas_call x1, Pallas kernels, body(): pl.pallas_call(kernel, out_shape=jax.ShapeDtypeStruct((2, 32, 4, *TILE),...  75.6 us
    unnamed x5, local copies, waits for them, and re-layouts  2.88 us

profile of v4, /device:TPU:32, one launch (start us, length us, event | category | flops | bytes accessed | tf_op | source)
XLA Modules:
  0.0 78.5 jit_solution(12584662060145649743)
XLA Ops:
  0.0 0.0 copy-start
  0.0 1.2 %copy-done = f32[2,32,1,1,4096]{4,3,2,1,0:T(1,128)S(1)} copy-done((f32[2,32,1,1,4096]{4,3,2,1,0:T(1,128)S(1)}, f32[2,32,1,1,4096]{4,3,2,1,0:T(1,128)}, u32[]{:S(2)}) %copy-start) | copy-done | bytes 1048600
  1.2 0.0 copy-start.1
  1.2 0.7 copy-done.1
  1.9 75.6 %shard_map.28 = f32[2,32,4,8,128]{4,3,2,1,0:T(8,128)S(1)} custom-call(f32[2,32,4,8,128]{4,3,2,1,0:T(8,128)S(1)} %bitcast.3, f32[4,4]{1,0:T(4,128)S(1)} %copy-done.1), custom_call_target="tpu_custom_call" | custom-call | tf_op jit(solution)/shard_map/pallas_call | solution.py:564
  77.5 1.0 %copy.5 = f32[2,32,1,1,4096]{4,3,2,1,0:T(1,128)} copy(f32[2,32,1,1,4096]{4,3,2,1,0:T(1,128)S(1)} %bitcast.2) | data formatting | bytes 2097152
Async XLA Ops:
  0.0 1.2 %copy-start = (f32[2,32,1,1,4096]{4,3,2,1,0:T(1,128)S(1)}, f32[2,32,1,1,4096]{4,3,2,1,0:T(1,128)}, u32[]{:S(2)}) copy-start(f32[2,32,1,1,4096]{4,3,2,1,0:T(1,128)} %param.2) | copy-start | bytes 3145732
  1.2 0.7 copy-start.1
